TPU v7x, 32 devices: a whole 2x2x4 slice. The times are simulated.
32 devices in a mesh: particle: 4 (over z), tile: 8 (over y, x, core).
Axes of the slice: x: 2, y: 2, z: 4, core: 2. Of those that a mesh axis runs over, the one named last changes fastest.
Arguments:
- biomass: float32 [16, 32768], P('particle', 'tile'), as said below
- water: float32 [16, 32768], P('particle', 'tile'), may hold values from -5 to 5
- flow_blocks: bfloat16 [256, 3, 128, 128], P('tile'), may hold values from -0.15625 to 0.15625
- neighbours: int32 [256, 3], P('tile'), may hold values from 0 to 255, as said below
- rain: float32 [4, 16, 32768], P(None, 'particle', 'tile'), may hold values from -4 to 4
- growth_rate: float32 [32768], P('tile'), may hold values from 0.05 to 0.5
- observations: float32 [2, 32768], P(None, 'tile'), may hold values from -5 to 5
- obs_precision: float32 [32768], P('tile'), as said below
- ancestors: int32 [2, 16], replicated, may hold values from 0 to 15
Outputs:
- means: float32 [2, 2, 32768], P(None, None, 'tile')
- biomass_out: float32 [16, 32768], P('particle', 'tile')
- water_out: float32 [16, 32768], P('particle', 'tile')
Inputs may be any that keep to these rules, and one draw needn't show every extreme that they name: `neighbours`: row n lists block n first, then one block 1 to 4 blocks below n and one 1 to 4 blocks above n, each clipped to the grid's ends. `biomass`: every entry lies between 0.5 and 2. `obs_precision`: every entry lies between 0.3 / sqrt(32768) and 3 / sqrt(32768).
All inputs are finite; a program needn't handle non-finite values.
Results may differ from a plain program's by a relative error of at most 0.0019.
Values may be sent and summed in bfloat16 or wider, within the bound.
No kernel may reach another device: no remote copies, remote signals or barrier semaphores. Data moves between devices by JAX's collectives and lax.ppermute only.
A program may use at most 64 MiB of HBM per device.

v0:
```python
import jax
import jax.numpy as jnp
from jax import lax
from jax.sharding import PartitionSpec as P

BLK = 128
CYCLES = 2
DAYS = 2
HALO = 4


def padded(cells, sides, width):
    for axis, dim in sides:
        count = lax.axis_size(axis)
        ends = count - 1
        head = lax.slice_in_dim(cells, 0, width, axis=dim)
        tail = lax.slice_in_dim(cells, cells.shape[dim] - width, cells.shape[dim], axis=dim)
        cells = jnp.concatenate(
            [
                lax.ppermute(tail, axis, [(i, (i + 1) % count) for i in range(ends)]),
                cells,
                lax.ppermute(head, axis, [((i + 1) % count, i) for i in range(ends)]),
            ],
            axis=dim,
        )
    return cells


def body(
    biomass,
    water,
    flow_blocks,
    neighbours,
    rain,
    growth_rate,
    observations,
    obs_precision,
    ancestors,
):
    part_dev = biomass.shape[0]
    cells = biomass.shape[1]
    blocks_dev = cells // BLK
    member = lax.axis_index("particle")
    tile_pos = lax.axis_index("tile")
    local_ids = neighbours - tile_pos * blocks_dev + HALO
    bio, wat = (biomass, water)
    collected = []
    for cycle in range(CYCLES):
        misfit_local = -0.5 * jnp.sum(obs_precision * (bio - observations[cycle]) ** 2, axis=1)
        summed = lax.psum(misfit_local, "tile")
        log_weight = lax.all_gather(summed, "particle", axis=0, tiled=True)
        shifted = jnp.exp(log_weight - jnp.max(log_weight))
        weight = shifted / jnp.sum(shifted)
        my_weight = lax.dynamic_slice_in_dim(weight, member * part_dev, part_dev)
        partial_sums = jnp.stack(
            [jnp.sum(my_weight[:, None] * bio, axis=0), jnp.sum(my_weight[:, None] * wat, axis=0)]
        )
        collected.append(lax.psum(partial_sums, "particle"))
        chosen = ancestors[cycle]
        mine = lax.dynamic_slice_in_dim(chosen, member * part_dev, part_dev)
        piece = (
            lax.all_gather(bio, "particle", axis=0, tiled=True),
            lax.all_gather(wat, "particle", axis=0, tiled=True),
        )
        count = piece[0].shape[0]
        hit = jnp.arange(count, dtype=jnp.int32)[None, :] == mine[:, None]
        bio, wat = tuple(
            (jnp.sum(jnp.where(hit[:, :, None], rows[None], 0.0), axis=1) for rows in piece)
        )
        for day in range(DAYS):
            wb = wat.astype(jnp.bfloat16).reshape(part_dev, blocks_dev, BLK)
            extended = padded(wb, (("tile", 1),), HALO)
            nearby = extended[:, local_ids]
            flux = jnp.einsum(
                "pnkc,nkdc->pnd", nearby, flow_blocks, preferred_element_type=jnp.float32
            ).reshape(part_dev, cells)
            wet = wat * wat / (1.0 + wat * wat)
            new_bio = bio + growth_rate * bio * (wet - 0.4 * bio)
            new_wat = wat + flux + rain[cycle * DAYS + day] - 0.2 * bio * wet
            bio = new_bio
            wat = new_wat
    return (jnp.stack(collected), bio, wat)


def solution(mesh):
    placed = (
        P("particle", "tile"),
        P("particle", "tile"),
        P("tile", None, None, None),
        P("tile", None),
        P(None, "particle", "tile"),
        P("tile"),
        P(None, "tile"),
        P("tile"),
        P(),
    )
    return jax.shard_map(
        body,
        mesh=mesh,
        in_specs=placed,
        out_specs=(P(None, None, "tile"), P("particle", "tile"), P("particle", "tile")),
        check_vma=False,
    )
```

profile of v0, /device:TPU:0, one launch (start us, length us, event | category | flops | bytes accessed | tf_op | source)
XLA Modules:
  0.0 191.6 jit_solution(2245552599224987325)
XLA Ops:
  7.2 0.8 fusion.25
  8.2 15.8 %all-gather = f32[4,4,4096]{2,1,0:T(4,128)S(1)} all-gather(f32[1,4,4096]{2,1,0:T(4,128)} %bitcast.146), channel_id=1, replica_groups=mesh['particle'=4,'tile'=8] {'particle'}, dimensions={0}, use_global_device_ids=true | all-gather | bytes 327680 | tf_op jit(solution)/shard_map/all_gather | solution.py:62
  24.1 0.8 reshape.145
  24.8 14.9 %all-gather.1 = f32[4,4,4096]{2,1,0:T(4,128)S(1)} all-gather(f32[1,4,4096]{2,1,0:T(4,128)} %bitcast.152), channel_id=1, replica_groups=mesh['particle'=4,'tile'=8] {'particle'}, dimensions={0}, use_global_device_ids=true | all-gather | bytes 327680 | tf_op jit(solution)/shard_map/all_gather | solution.py:63
  39.7 0.8 reshape.147
  40.5 1.5 select_reduce_fusion.3
  42.0 1.3 collective-permute-start
  43.3 1.3 collective-permute-start.1
  44.6 0.7 compare_select_fusion
  45.5 0.9 fusion.24
  47.1 1.2 dynamic-slice.2
  49.1 1.3 gather_fusion
  50.4 2.9 %multiply_reduce_fusion.5 = (f32[4]{0:T(128)S(1)}, f32[4]{0:T(128)S(1)}, f32[4,4096]{1,0:T(4,128)}, f32[4,4096]{1,0:T(4,128)}, f32[32,4,128,1]{2,1,3,0:T(4,128)S(1)}) fusion(f32[4,4096]{1,0:T(4,128)} %param.9, f32[4096]{0:T(1024)S(1)} %bitcast.156, f32[4096]{0:T(1024)} %param.16, f32[4096]{0:T(1024)S(1)} %bitcast.155, f32[4,4096]{1,0:T(4,128)S(1)} %get-tuple-element.11, ...), kind=kOutput, calls=%fused_computation.50 | convolution fusion | flops 13058040 | bytes 3768352 | tf_op jit(solution)/shard_map/pnkc,nkdc->pnd/dot_general | solution.py:74
  53.4 0.9 fusion.14
  54.9 4.7 %collective-permute-start.2 = (bf16[4,4,128]{2,0,1:T(4,128)(2,1)}, bf16[4,4,128]{2,0,1:T(4,128)(2,1)S(1)}, u32[]{:S(2)}, u32[]{:S(2)}) collective-permute-start(bf16[4,4,128]{2,0,1:T(4,128)(2,1)} %get-tuple-element.27), channel_id=1, source_target_pairs={{0,1},{1,2},{2,3},{3,4},{4,5},{5,6},{6,7},{8,9},{9,10},{10,11},{11... | collective-permute-start | bytes 12296 | tf_op jit(solution)/shard_map/ppermute | solution.py:20
  59.6 1.3 collective-permute-start.3
  61.0 15.7 %all-reduce.2 = (f32[4]{0:T(128)S(1)}, f32[4]{0:T(128)S(1)}) all-reduce(f32[4]{0:T(128)S(1)} %get-tuple-element.38, f32[4]{0:T(128)S(1)} %get-tuple-element.39), channel_id=1, replica_groups=mesh['particle'=4,'tile'=8] {'tile'}, use_global_device_ids=true, to_apply=%region_10.11 | all-reduce | flops 8 | bytes 64 | tf_op jit(solution)/shard_map/psum | solution.py:50
  77.1 11.5 %all-reduce.4 = (f32[16]{0:T(128)S(1)}, f32[16]{0:T(128)S(1)}) all-reduce(f32[16]{0:T(128)S(1)} %dynamic-update-slice.1, f32[16]{0:T(128)S(1)} %dynamic-update-slice), channel_id=1, replica_groups=mesh['particle'=4,'tile'=8] {'particle'}, use_global_device_ids=true, to_apply=%add.1 | all-reduce | flops 32 | bytes 256
  88.6 0.7 reduce_max.19
  89.3 1.4 fusion.17
  90.7 1.4 broadcast_divide_fusion
  92.0 0.7 reduce_max.18
  92.7 1.4 fusion.16
  94.1 1.4 broadcast_divide_fusion.1
  95.6 0.7 multiply_reduce_fusion.4
  96.3 14.1 %all-gather.2 = f32[4,4,4096]{2,1,0:T(4,128)S(1)} all-gather(f32[1,4,4096]{2,1,0:T(4,128)} %bitcast.145), channel_id=1, replica_groups=mesh['particle'=4,'tile'=8] {'particle'}, dimensions={0}, use_global_device_ids=true | all-gather | bytes 327680 | tf_op jit(solution)/shard_map/all_gather | solution.py:62
  110.4 0.7 dynamic_slice.14
  111.1 0.8 reshape.149
  111.9 0.8 pad_maximum_fusion.2
  112.7 0.7 gather_fusion.1
  113.4 2.1 %multiply_reduce_fusion.1 = (f32[4096]{0:T(1024)S(1)}, f32[4096]{0:T(1024)S(1)}, f32[4,4096]{1,0:T(4,128)S(1)}) fusion(f32[4,4096]{1,0:T(4,128)} %get-tuple-element.21, f32[4]{0:T(128)} %dynamic_slice.14, f32[4,4096]{1,0:T(4,128)} %get-tuple-element.22, f32[4,4096]{1,0:T(4,128)S(1)} %get-tuple-element.11, f32[4,4096]{1,0:T(4,128)S(1)} %get-tuple-element.12, ...), kind=kOutput, calls=%fused_computation.44 | convolution fusion | flops 12902400 | bytes 3686416 | tf_op jit(solution)/shard_map/pnkc,nkdc->pnd/dot_general | solution.py:74
  115.5 13.8 %all-gather.3 = f32[4,4,4096]{2,1,0:T(4,128)S(1)} all-gather(f32[1,4,4096]{2,1,0:T(4,128)S(1)} %bitcast.151), channel_id=1, replica_groups=mesh['particle'=4,'tile'=8] {'particle'}, dimensions={0}, use_global_device_ids=true | all-gather | bytes 327680 | tf_op jit(solution)/shard_map/all_gather | solution.py:63
  129.3 0.8 reshape.151
  130.1 1.5 select_reduce_fusion.1
  131.6 1.3 collective-permute-start.4
  132.9 1.3 collective-permute-start.5
  134.2 1.4 maximum_bitcast_fusion
  135.6 0.9 collective-permute-done.5
  136.5 0.7 gather_fusion.2
  137.2 2.7 %multiply_add_fusion = (f32[4,4096]{1,0:T(4,128)}, f32[4,4096]{1,0:T(4,128)S(1)}, f32[32,4,128,1]{2,1,3,0:T(4,128)S(1)}) fusion(f32[4096]{0:T(1024)S(1)} %copy-done.2, f32[4,4096]{1,0:T(4,128)S(1)} %get-tuple-element.5, f32[4,4096]{1,0:T(4,128)S(1)} %get-tuple-element.6, f32[4,4,4096]{2,1,0:T(4,128)} %param.13, bf16[4,32,3,128]{3,0,2,1:T(4,128)(2,1)S(1)} %bitcast.150, ...), kind=kOutput, calls=%fused_computation.41 | convolution fusion | flops 12926976 | bytes 3653632 | tf_op jit(solution)/shard_map/pnkc,nkdc->pnd/dot_general | solution.py:74
  139.9 0.9 fusion.15
  140.8 4.3 %collective-permute-start.6 = (bf16[4,4,128]{2,0,1:T(4,128)(2,1)S(1)}, bf16[4,4,128]{2,0,1:T(4,128)(2,1)S(1)}, u32[]{:S(2)}, u32[]{:S(2)}) collective-permute-start(bf16[4,4,128]{2,0,1:T(4,128)(2,1)S(1)} %get-tuple-element.23), channel_id=1, source_target_pairs={{0,1},{1,2},{2,3},{3,4},{4,5},{5,6},{6,7},{8,9},{9,10},{10,11},{11... | collective-permute-start | bytes 12296 | tf_op jit(solution)/shard_map/ppermute | solution.py:20
  145.1 1.3 collective-permute-start.7
  147.1 1.8 collective-permute-done.7
  149.0 0.7 gather_fusion.3
  149.7 2.7 %fusion.2 = f32[4,4096]{1,0:T(4,128)} fusion(f32[4,4096]{1,0:T(4,128)S(1)} %get-tuple-element.20, bf16[4,32,3,128]{3,0,2,1:T(4,128)(2,1)S(1)} %bitcast.147, bf16[32,3,128,128]{3,2,1,0:T(8,128)(2,1)S(1)} %copy-done, f32[4,4,4096]{2,1,0:T(4,128)} %param.13, f32[4,4096]{1,0:T(4,128)S(1)} %get-tuple-element.5, f32[4,4096]{1,0:T(4,128)S(1)} %get-tuple-element.6, ...), kind=kOutput, calls=%fused_computation.7 | convolution fusion | flops 12845056 | bytes 3588096 | tf_op jit(solution)/shard_map/pnkc,nkdc->pnd/dot_general | solution.py:74
  152.3 31.0 %all-reduce.7.cloned.1.call-done = (f32[1,2,4096]{2,1,0:T(2,128)}, f32[1,2,4096]{2,1,0:T(2,128)}) async-done(((f32[1,2,4096]{2,1,0:T(2,128)}, f32[1,2,4096]{2,1,0:T(2,128)}), (f32[1,2,4096]{2,1,0:T(2,128)}, f32[1,2,4096]{2,1,0:T(2,128)})) %all-reduce.7.cloned.1.call-update) | async-done | bytes 65552 | tf_op jit(solution)/shard_map/psum | solution.py:58
  183.4 1.4 pad_maximum_fusion
  (43 shorter events, 3.1 us)
Async XLA Ops:
  7.2 43.3 %copy-start = (bf16[32,3,128,128]{3,2,1,0:T(8,128)(2,1)S(1)}, bf16[32,3,128,128]{3,2,1,0:T(8,128)(2,1)}, u32[]{:S(2)}) copy-start(bf16[32,3,128,128]{3,2,1,0:T(8,128)(2,1)} %param.11) | copy-start | bytes 9437188
  7.2 176.2 %all-reduce.7.cloned.1.call-start = ((), (), s32[]{:S(2)}) async-start(), calls=%async_computation | async-start | bytes 131072 | tf_op jit(solution)/shard_map/psum | solution.py:58
  24.8 70.7 %copy-start.1 = (f32[4,4096]{1,0:T(4,128)S(1)}, f32[4,4096]{1,0:T(4,128)}, u32[]{:S(2)}) copy-start(f32[4,4096]{1,0:T(4,128)} %param.9) | copy-start | bytes 196612
  24.8 70.7 %copy-start.3 = (f32[4,4096]{1,0:T(4,128)S(1)}, f32[4,4096]{1,0:T(4,128)}, u32[]{:S(2)}) copy-start(f32[4,4096]{1,0:T(4,128)} %param.10) | copy-start | bytes 196612
  42.0 7.0 %collective-permute-start = (bf16[4,4,128]{2,0,1:T(4,128)(2,1)S(1)}, bf16[4,4,128]{2,0,1:T(4,128)(2,1)S(1)}, u32[]{:S(2)}, u32[]{:S(2)}) collective-permute-start(bf16[4,4,128]{2,0,1:T(4,128)(2,1)S(1)} %get-tuple-element.29), channel_id=1, source_target_pairs={{0,1},{1,2},{2,3},{3,4},{4,5},{5,6},{6,7},{8,9},{9,10},{10,11},{11... | collective-permute-start | bytes 12296 | tf_op jit(solution)/shard_map/ppermute | solution.py:20
  43.3 5.7 %collective-permute-start.1 = (bf16[4,4,128]{2,0,1:T(4,128)(2,1)S(1)}, bf16[4,4,128]{2,0,1:T(4,128)(2,1)S(1)}, u32[]{:S(2)}, u32[]{:S(2)}) collective-permute-start(bf16[4,4,128]{2,0,1:T(4,128)(2,1)S(1)} %get-tuple-element.30), channel_id=1, source_target_pairs={{1,0},{2,1},{3,2},{4,3},{5,4},{6,5},{7,6},{9,8},{10,9},{11,10},{12... | collective-permute-start | bytes 12296 | tf_op jit(solution)/shard_map/ppermute | solution.py:22
  54.3 42.0 %copy-start.4 = (bf16[4,32,128]{2,0,1:T(4,128)(2,1)}, bf16[4,32,128]{2,0,1:T(4,128)(2,1)S(1)}, u32[]{:S(2)}) copy-start(bf16[4,32,128]{2,0,1:T(4,128)(2,1)S(1)} %fusion.14) | copy-start | bytes 98308
  54.9 57.0 %collective-permute-start.2 = (bf16[4,4,128]{2,0,1:T(4,128)(2,1)}, bf16[4,4,128]{2,0,1:T(4,128)(2,1)S(1)}, u32[]{:S(2)}, u32[]{:S(2)}) collective-permute-start(bf16[4,4,128]{2,0,1:T(4,128)(2,1)} %get-tuple-element.27), channel_id=1, source_target_pairs={{0,1},{1,2},{2,3},{3,4},{4,5},{5,6},{6,7},{8,9},{9,10},{10,11},{11... | collective-permute-start | bytes 12296 | tf_op jit(solution)/shard_map/ppermute | solution.py:20
  59.6 52.2 %collective-permute-start.3 = (bf16[4,4,128]{2,0,1:T(4,128)(2,1)}, bf16[4,4,128]{2,0,1:T(4,128)(2,1)}, u32[]{:S(2)}, u32[]{:S(2)}) collective-permute-start(bf16[4,4,128]{2,0,1:T(4,128)(2,1)} %get-tuple-element.28), channel_id=1, source_target_pairs={{1,0},{2,1},{3,2},{4,3},{5,4},{6,5},{7,6},{9,8},{10,9},{11,10},{12... | collective-permute-start | bytes 12296 | tf_op jit(solution)/shard_map/ppermute | solution.py:22
  111.8 22.4 %copy-start.5 = (f32[4096]{0:T(1024)S(1)}, f32[4096]{0:T(1024)}, u32[]{:S(2)}) copy-start(f32[4096]{0:T(1024)} %get-tuple-element.7) | copy-start | bytes 49156
  111.8 25.4 %copy-start.2 = (f32[4096]{0:T(1024)S(1)}, f32[4096]{0:T(1024)}, u32[]{:S(2)}) copy-start(f32[4096]{0:T(1024)} %param.14) | copy-start | bytes 49156
  131.6 4.0 %collective-permute-start.4 = (bf16[4,4,128]{2,0,1:T(4,128)(2,1)S(1)}, bf16[4,4,128]{2,0,1:T(4,128)(2,1)S(1)}, u32[]{:S(2)}, u32[]{:S(2)}) collective-permute-start(bf16[4,4,128]{2,0,1:T(4,128)(2,1)S(1)} %get-tuple-element.25), channel_id=1, source_target_pairs={{0,1},{1,2},{2,3},{3,4},{4,5},{5,6},{6,7},{8,9},{9,10},{10,11},{11... | collective-permute-start | bytes 12296 | tf_op jit(solution)/shard_map/ppermute | solution.py:20
  132.9 3.5 %collective-permute-start.5 = (bf16[4,4,128]{2,0,1:T(4,128)(2,1)S(1)}, bf16[4,4,128]{2,0,1:T(4,128)(2,1)S(1)}, u32[]{:S(2)}, u32[]{:S(2)}) collective-permute-start(bf16[4,4,128]{2,0,1:T(4,128)(2,1)S(1)} %get-tuple-element.26), channel_id=1, source_target_pairs={{1,0},{2,1},{3,2},{4,3},{5,4},{6,5},{7,6},{9,8},{10,9},{11,10},{12... | collective-permute-start | bytes 12296 | tf_op jit(solution)/shard_map/ppermute | solution.py:22
  140.8 6.3 %collective-permute-start.6 = (bf16[4,4,128]{2,0,1:T(4,128)(2,1)S(1)}, bf16[4,4,128]{2,0,1:T(4,128)(2,1)S(1)}, u32[]{:S(2)}, u32[]{:S(2)}) collective-permute-start(bf16[4,4,128]{2,0,1:T(4,128)(2,1)S(1)} %get-tuple-element.23), channel_id=1, source_target_pairs={{0,1},{1,2},{2,3},{3,4},{4,5},{5,6},{6,7},{8,9},{9,10},{10,11},{11... | collective-permute-start | bytes 12296 | tf_op jit(solution)/shard_map/ppermute | solution.py:20
  145.1 3.8 %collective-permute-start.7 = (bf16[4,4,128]{2,0,1:T(4,128)(2,1)S(1)}, bf16[4,4,128]{2,0,1:T(4,128)(2,1)S(1)}, u32[]{:S(2)}, u32[]{:S(2)}) collective-permute-start(bf16[4,4,128]{2,0,1:T(4,128)(2,1)S(1)} %get-tuple-element.24), channel_id=1, source_target_pairs={{1,0},{2,1},{3,2},{4,3},{5,4},{6,5},{7,6},{9,8},{10,9},{11,10},{12... | collective-permute-start | bytes 12296 | tf_op jit(solution)/shard_map/ppermute | solution.py:22
Sparse Core Ops, SparseCore 0:
  147.2 36.1 all-reduce.6
where the time goes:
time: 193 us; the launch traced here: 192 us
  blocking collectives  85.8 us (44%)
  waiting for transfers between devices  33.8 us (18%)
  other arithmetic  18.2 us (9%)
  starting transfers between devices  16.8 us (9%)
  between operations  15 us (8%)
  local copies, waits for them, and re-layouts  11.7 us (6%)
  matrix products  10.5 us (5%)
    psum x1, waiting for transfers between devices, body(): collected.append(lax.psum(partial_sums, 'particle'))  31 us
    all_gather x2, blocking collectives, body(): lax.all_gather(bio, 'particle', axis=0, tiled=True)  29.9 us
    all_gather x2, blocking collectives, body(): lax.all_gather(wat, 'particle', axis=0, tiled=True)  28.7 us
    psum x1, blocking collectives, body(): summed = lax.psum(misfit_local, 'tile')  15.7 us
    ppermute x4, starting transfers between devices, padded(): lax.ppermute(tail, axis, [(i, (i + 1) % count) for i in range(ends)])  11.6 us
    unnamed x1, blocking collectives  11.5 us
    dot_general x4, matrix products, body(): jnp.einsum('pnkc,nkdc->pnd', nearby, flow_blocks, preferred_element_type=...  10.5 us
    ppermute x4, starting transfers between devices, padded(): lax.ppermute(head, axis, [((i + 1) % count, i) for i in range(ends)])  5.17 us
  transfers between devices with their start and end apart: 9, of which 3 were waited for; matrix products, arithmetic and copies ran while one was open for 10% of the time, Pallas kernels for 0%

commit v1 on v0

--- a/solution.py
+++ b/solution.py
@@ -58,10 +58,24 @@
         collected.append(lax.psum(partial_sums, "particle"))
         chosen = ancestors[cycle]
         mine = lax.dynamic_slice_in_dim(chosen, member * part_dev, part_dev)
-        piece = (
-            lax.all_gather(bio, "particle", axis=0, tiled=True),
-            lax.all_gather(wat, "particle", axis=0, tiled=True),
-        )
+
+        def values_report(xs):
+            q_next = lax.axis_index("particle")
+            u_next = lax.axis_size("particle")
+            z_new, v_next = (u_next, q_next)
+            x_new, after = (xs, 1)
+            while after < z_new:
+                crops = []
+                for j in tuple(range(z_new)):
+                    crops.append((j, j ^ after))
+                plain = lax.ppermute(x_new, "particle", crops)
+                a_next = jnp.concatenate([x_new, plain], axis=0)
+                r1 = jnp.concatenate([plain, x_new], axis=0)
+                x_new = jnp.where(v_next & after == 0, a_next, r1)
+                after = 2 * after
+            return x_new
+
+        piece = (values_report(bio), lax.all_gather(wat, "particle", axis=0, tiled=True))
         count = piece[0].shape[0]
         hit = jnp.arange(count, dtype=jnp.int32)[None, :] == mine[:, None]
         bio, wat = tuple(

time: 193 us -> 170 us (0.88)
  blocking collectives: 85.8 us -> 54.7 us
  waiting for transfers between devices: 33.8 us -> 40.6 us
  other arithmetic: 18.2 us -> 20.2 us
    all_gather x2 -> x0, blocking collectives: 29.9 us -> none  [body(): lax.all_gather(bio, 'particle', axis=0, tiled=True)]
    ppermute x0 -> x4, waiting for transfers between devices: none -> 7.32 us  [values_report(): plain = lax.ppermute(x_new, 'particle', crops)]
    ppermute x0 -> x4, starting transfers between devices: none -> 4.22 us  [values_report(): plain = lax.ppermute(x_new, 'particle', crops)]
    select_n x0 -> x4, other arithmetic: none -> 3.75 us  [values_report(): x_new = jnp.where(v_next & after == 0, a_next, r1)]
    psum x1, waiting for transfers between devices: 31 us -> 27.4 us  [body(): collected.append(lax.psum(partial_sums, 'particle'))]
    ppermute x4, starting transfers between devices: 11.6 us -> 8.14 us  [padded(): lax.ppermute(tail, axis, [(i, (i + 1) % count) for i in range(ends)])]
    ppermute x4, waiting for transfers between devices: 2.73 us -> 5.84 us  [padded(): lax.ppermute(head, axis, [((i + 1) % count, i) for i in range(ends)])]
    unnamed x21 -> x13, local copies, waits for them, and re-layouts: 4.85 us -> 3.26 us
  transfers between devices with their start and end apart: 9 -> 13, of which waited for: 3 -> 5; matrix products, arithmetic and copies ran while one was open for 10% -> 11% of each run, Pallas kernels for 0% -> 0%
where the time goes in v1:
time: 170 us; the launch traced here: 169 us
  blocking collectives  54.7 us (32%)
  waiting for transfers between devices  40.6 us (24%)
  other arithmetic  20.2 us (12%)
  starting transfers between devices  17.6 us (10%)
  between operations  14.9 us (9%)
  matrix products  11 us (6%)
  local copies, waits for them, and re-layouts  9.95 us (6%)
    all_gather x2, blocking collectives, body(): lax.all_gather(wat, 'particle', axis=0, tiled=True)  30.6 us
    psum x1, waiting for transfers between devices, body(): collected.append(lax.psum(partial_sums, 'particle'))  27.4 us
    psum x1, blocking collectives, body(): summed = lax.psum(misfit_local, 'tile')  14.2 us
    dot_general x4, matrix products, body(): jnp.einsum('pnkc,nkdc->pnd', nearby, flow_blocks, preferred_element_type=...  11 us
    unnamed x1, blocking collectives  9.96 us
    ppermute x4, starting transfers between devices, padded(): lax.ppermute(tail, axis, [(i, (i + 1) % count) for i in range(ends)])  8.14 us
    ppermute x4, waiting for transfers between devices, values_report(): plain = lax.ppermute(x_new, 'particle', crops)  7.32 us
    ppermute x4, waiting for transfers between devices, padded(): lax.ppermute(head, axis, [((i + 1) % count, i) for i in range(ends)])  5.84 us
  transfers between devices with their start and end apart: 13, of which 5 were waited for; matrix products, arithmetic and copies ran while one was open for 11% of the time, Pallas kernels for 0%

profile of v1, /device:TPU:0, one launch (start us, length us, event | category | flops | bytes accessed | tf_op | source)
XLA Modules:
  0.0 169.0 jit_solution(7645181512215862912)
XLA Ops:
  7.2 3.1 %collective-permute-start = (f32[4,4096]{1,0:T(4,128)}, f32[4,4096]{1,0:T(4,128)S(1)}, u32[]{:S(2)}, u32[]{:S(2)}) collective-permute-start(f32[4,4096]{1,0:T(4,128)} %param.9), channel_id=1, source_target_pairs={{0,8},{8,0},{16,24},{24,16},{1,9},{9,1},{17,25},{25,17},{2,10},{10... | collective-permute-start | bytes 196616 | tf_op jit(solution)/shard_map/ppermute | solution.py:71
  10.3 0.8 fusion.25
  11.2 0.7 compare_select_fusion
  12.1 1.5 fusion.24
  13.6 14.3 %all-gather = f32[4,4,4096]{2,1,0:T(4,128)S(1)} all-gather(f32[1,4,4096]{2,1,0:T(4,128)} %bitcast.148), channel_id=1, replica_groups=mesh['particle'=4,'tile'=8] {'particle'}, dimensions={0}, use_global_device_ids=true | all-gather | bytes 327680 | tf_op jit(solution)/shard_map/all_gather | solution.py:78
  27.9 0.8 reshape.233
  28.8 1.0 maximum_select_fusion.2
  29.8 0.7 collective-permute-start.1
  30.6 6.5 %collective-permute-done.1 = f32[8,4096]{1,0:T(8,128)S(1)} collective-permute-done((f32[8,4096]{1,0:T(8,128)S(1)}, f32[8,4096]{1,0:T(8,128)S(1)}, u32[]{:S(2)}, u32[]{:S(2)}) %collective-permute-start.1) | collective-permute-done | bytes 131104 | tf_op jit(solution)/shard_map/ppermute | solution.py:71
  37.1 1.4 select_reduce_fusion.3
  38.6 1.3 collective-permute-start.2
  39.9 1.3 collective-permute-start.3
  41.2 1.2 dynamic-slice.2
  43.1 1.6 collective-permute-done.3
  44.7 1.3 gather_fusion
  46.0 3.0 %multiply_reduce_fusion.5 = (f32[4]{0:T(128)S(1)}, f32[4]{0:T(128)S(1)}, f32[4,4096]{1,0:T(4,128)S(1)}, f32[4,4096]{1,0:T(4,128)S(1)}, f32[32,4,128,1]{2,1,3,0:T(4,128)}) fusion(f32[4,4096]{1,0:T(4,128)} %param.9, f32[4096]{0:T(1024)} %bitcast.150, f32[4096]{0:T(1024)} %param.16, f32[4096]{0:T(1024)} %bitcast.149, f32[4,4096]{1,0:T(4,128)S(1)} %get-tuple-element.11, ...), kind=kOutput, calls=%fused_computation.54 | convolution fusion | flops 13058040 | bytes 3768352 | tf_op jit(solution)/shard_map/pnkc,nkdc->pnd/dot_general | solution.py:88
  49.0 14.2 %all-reduce.2 = (f32[4]{0:T(128)S(1)}, f32[4]{0:T(128)S(1)}) all-reduce(f32[4]{0:T(128)S(1)} %get-tuple-element.38, f32[4]{0:T(128)S(1)} %get-tuple-element.39), channel_id=1, replica_groups=mesh['particle'=4,'tile'=8] {'tile'}, use_global_device_ids=true, to_apply=%region_10.11 | all-reduce | flops 8 | bytes 64 | tf_op jit(solution)/shard_map/psum | solution.py:50
  63.6 10.0 %all-reduce.4 = (f32[16]{0:T(128)S(1)}, f32[16]{0:T(128)S(1)}) all-reduce(f32[16]{0:T(128)S(1)} %dynamic-update-slice.1, f32[16]{0:T(128)S(1)} %dynamic-update-slice), channel_id=1, replica_groups=mesh['particle'=4,'tile'=8] {'particle'}, use_global_device_ids=true, to_apply=%add.1 | all-reduce | flops 32 | bytes 256
  74.2 1.2 fusion.16
  75.4 1.3 broadcast_divide_fusion.1
  77.3 1.3 fusion.17
  78.7 1.0 multiply_reduce_fusion.4
  79.7 0.9 fusion.14
  80.6 1.3 collective-permute-start.4
  81.9 1.3 collective-permute-start.5
  83.7 0.6 maximum_bitcast_fusion
  84.3 1.3 broadcast_divide_fusion
  86.2 0.7 gather_fusion.1
  86.9 0.8 collective-permute-done.6
  87.7 1.6 maximum_select_fusion.3
  89.3 2.7 %multiply_reduce_fusion.1 = (f32[4096]{0:T(1024)}, f32[4096]{0:T(1024)}, f32[4,4096]{1,0:T(4,128)S(1)}) fusion(f32[4,4096]{1,0:T(4,128)S(1)} %get-tuple-element.21, f32[4]{0:T(128)} %dynamic_slice.14, f32[4,4096]{1,0:T(4,128)S(1)} %get-tuple-element.22, f32[4,4096]{1,0:T(4,128)S(1)} %get-tuple-element.11, f32[4,4096]{1,0:T(4,128)S(1)} %get-tuple-element.12, ...), kind=kOutput, calls=%fused_computation.48 | convolution fusion | flops 12902400 | bytes 3686416 | tf_op jit(solution)/shard_map/pnkc,nkdc->pnd/dot_general | solution.py:88
  92.0 16.2 %all-gather.1 = f32[4,4,4096]{2,1,0:T(4,128)S(1)} all-gather(f32[1,4,4096]{2,1,0:T(4,128)S(1)} %bitcast.147), channel_id=1, replica_groups=mesh['particle'=4,'tile'=8] {'particle'}, dimensions={0}, use_global_device_ids=true | all-gather | bytes 327680 | tf_op jit(solution)/shard_map/all_gather | solution.py:78
  108.3 0.8 reshape.235
  109.0 1.1 maximum_select_fusion.1
  110.2 1.4 select_reduce_fusion.1
  111.6 1.3 collective-permute-start.8
  112.9 1.3 collective-permute-start.9
  114.2 1.4 maximum_bitcast_fusion.1
  115.7 4.3 %collective-permute-done.9 = bf16[4,4,128]{2,0,1:T(4,128)(2,1)S(1)} collective-permute-done((bf16[4,4,128]{2,0,1:T(4,128)(2,1)S(1)}, bf16[4,4,128]{2,0,1:T(4,128)(2,1)S(1)}, u32[]{:S(2)}, u32[]{:S(2)}) %collective-permute-start.9) | collective-permute-done | bytes 4128 | tf_op jit(solution)/shard_map/ppermute | solution.py:22
  120.0 0.7 gather_fusion.2
  120.7 2.7 %multiply_add_fusion = (f32[4,4096]{1,0:T(4,128)}, f32[4,4096]{1,0:T(4,128)S(1)}, f32[32,4,128,1]{2,1,3,0:T(4,128)S(1)}) fusion(f32[4096]{0:T(1024)} %param.14, f32[4,4096]{1,0:T(4,128)S(1)} %get-tuple-element.5, f32[4,4096]{1,0:T(4,128)S(1)} %get-tuple-element.6, f32[4,4,4096]{2,1,0:T(4,128)} %param.13, bf16[4,32,3,128]{3,0,2,1:T(4,128)(2,1)S(1)} %bitcast.146, ...), kind=kOutput, calls=%fused_computation.45 | convolution fusion | flops 12926976 | bytes 3653632 | tf_op jit(solution)/shard_map/pnkc,nkdc->pnd/dot_general | solution.py:88
  123.4 0.9 fusion.15
  124.3 4.3 %collective-permute-start.10 = (bf16[4,4,128]{2,0,1:T(4,128)(2,1)S(1)}, bf16[4,4,128]{2,0,1:T(4,128)(2,1)S(1)}, u32[]{:S(2)}, u32[]{:S(2)}) collective-permute-start(bf16[4,4,128]{2,0,1:T(4,128)(2,1)S(1)} %get-tuple-element.23), channel_id=1, source_target_pairs={{0,1},{1,2},{2,3},{3,4},{4,5},{5,6},{6,7},{8,9},{9,10},{10,11},{11... | collective-permute-start | bytes 12296 | tf_op jit(solution)/shard_map/ppermute | solution.py:20
  128.6 1.3 collective-permute-start.11
  129.9 27.4 %all-reduce.7.cloned.1.call-done = (f32[1,2,4096]{2,1,0:T(2,128)}, f32[1,2,4096]{2,1,0:T(2,128)}) async-done(((f32[1,2,4096]{2,1,0:T(2,128)}, f32[1,2,4096]{2,1,0:T(2,128)}), (f32[1,2,4096]{2,1,0:T(2,128)}, f32[1,2,4096]{2,1,0:T(2,128)})) %all-reduce.7.cloned.1.call-update) | async-done | bytes 65552 | tf_op jit(solution)/shard_map/psum | solution.py:58
  157.2 1.4 pad_maximum_fusion
  158.7 0.7 gather_fusion.3
  159.4 2.7 %fusion.2 = f32[4,4096]{1,0:T(4,128)} fusion(f32[4,4096]{1,0:T(4,128)S(1)} %get-tuple-element.20, bf16[4,32,3,128]{3,0,2,1:T(4,128)(2,1)S(1)} %bitcast.143, bf16[32,3,128,128]{3,2,1,0:T(8,128)(2,1)S(1)} %copy-done, f32[4,4,4096]{2,1,0:T(4,128)} %param.13, f32[4,4096]{1,0:T(4,128)S(1)} %get-tuple-element.5, f32[4,4096]{1,0:T(4,128)S(1)} %get-tuple-element.6, ...), kind=kOutput, calls=%fused_computation.7 | convolution fusion | flops 12845056 | bytes 3588096 | tf_op jit(solution)/shard_map/pnkc,nkdc->pnd/dot_general | solution.py:88
  (45 shorter events, 3.5 us)
Async XLA Ops:
  7.2 38.9 %copy-start = (bf16[32,3,128,128]{3,2,1,0:T(8,128)(2,1)S(1)}, bf16[32,3,128,128]{3,2,1,0:T(8,128)(2,1)}, u32[]{:S(2)}) copy-start(bf16[32,3,128,128]{3,2,1,0:T(8,128)(2,1)} %param.11) | copy-start | bytes 9437188
  7.2 150.1 %all-reduce.7.cloned.1.call-start = ((), (), s32[]{:S(2)}) async-start(), calls=%async_computation | async-start | bytes 131072 | tf_op jit(solution)/shard_map/psum | solution.py:58
  7.2 21.6 %collective-permute-start = (f32[4,4096]{1,0:T(4,128)}, f32[4,4096]{1,0:T(4,128)S(1)}, u32[]{:S(2)}, u32[]{:S(2)}) collective-permute-start(f32[4,4096]{1,0:T(4,128)} %param.9), channel_id=1, source_target_pairs={{0,8},{8,0},{16,24},{24,16},{1,9},{9,1},{17,25},{25,17},{2,10},{10... | collective-permute-start | bytes 196616 | tf_op jit(solution)/shard_map/ppermute | solution.py:71
  27.9 50.8 %copy-start.1 = (f32[4,4096]{1,0:T(4,128)S(1)}, f32[4,4096]{1,0:T(4,128)}, u32[]{:S(2)}) copy-start(f32[4,4096]{1,0:T(4,128)} %param.9) | copy-start | bytes 196612
  29.8 7.3 %collective-permute-start.1 = (f32[8,4096]{1,0:T(8,128)S(1)}, f32[8,4096]{1,0:T(8,128)S(1)}, u32[]{:S(2)}, u32[]{:S(2)}) collective-permute-start(f32[8,4096]{1,0:T(8,128)S(1)} %maximum_select_fusion.2), channel_id=1, source_target_pairs={{0,16},{8,24},{16,0},{24,8},{1,17},{9,25},{17,1},{25,9},{2,18},{10... | collective-permute-start | bytes 393224 | tf_op jit(solution)/shard_map/ppermute | solution.py:71
  38.6 4.5 %collective-permute-start.2 = (bf16[4,4,128]{2,0,1:T(4,128)(2,1)S(1)}, bf16[4,4,128]{2,0,1:T(4,128)(2,1)S(1)}, u32[]{:S(2)}, u32[]{:S(2)}) collective-permute-start(bf16[4,4,128]{2,0,1:T(4,128)(2,1)S(1)} %get-tuple-element.29), channel_id=1, source_target_pairs={{0,1},{1,2},{2,3},{3,4},{4,5},{5,6},{6,7},{8,9},{9,10},{10,11},{11... | collective-permute-start | bytes 12296 | tf_op jit(solution)/shard_map/ppermute | solution.py:20
  39.9 4.8 %collective-permute-start.3 = (bf16[4,4,128]{2,0,1:T(4,128)(2,1)S(1)}, bf16[4,4,128]{2,0,1:T(4,128)(2,1)S(1)}, u32[]{:S(2)}, u32[]{:S(2)}) collective-permute-start(bf16[4,4,128]{2,0,1:T(4,128)(2,1)S(1)} %get-tuple-element.30), channel_id=1, source_target_pairs={{1,0},{2,1},{3,2},{4,3},{5,4},{6,5},{7,6},{9,8},{10,9},{11,10},{12... | collective-permute-start | bytes 12296 | tf_op jit(solution)/shard_map/ppermute | solution.py:22
  80.6 5.5 %collective-permute-start.4 = (bf16[4,4,128]{2,0,1:T(4,128)(2,1)S(1)}, bf16[4,4,128]{2,0,1:T(4,128)(2,1)S(1)}, u32[]{:S(2)}, u32[]{:S(2)}) collective-permute-start(bf16[4,4,128]{2,0,1:T(4,128)(2,1)S(1)} %get-tuple-element.27), channel_id=1, source_target_pairs={{0,1},{1,2},{2,3},{3,4},{4,5},{5,6},{6,7},{8,9},{9,10},{10,11},{11... | collective-permute-start | bytes 12296 | tf_op jit(solution)/shard_map/ppermute | solution.py:20
  81.9 4.2 %collective-permute-start.5 = (bf16[4,4,128]{2,0,1:T(4,128)(2,1)S(1)}, bf16[4,4,128]{2,0,1:T(4,128)(2,1)S(1)}, u32[]{:S(2)}, u32[]{:S(2)}) collective-permute-start(bf16[4,4,128]{2,0,1:T(4,128)(2,1)S(1)} %get-tuple-element.28), channel_id=1, source_target_pairs={{1,0},{2,1},{3,2},{4,3},{5,4},{6,5},{7,6},{9,8},{10,9},{11,10},{12... | collective-permute-start | bytes 12296 | tf_op jit(solution)/shard_map/ppermute | solution.py:22
  83.2 4.4 %collective-permute-start.6 = (f32[4,4096]{1,0:T(4,128)S(1)}, f32[4,4096]{1,0:T(4,128)}, u32[]{:S(2)}, u32[]{:S(2)}) collective-permute-start(f32[4,4096]{1,0:T(4,128)S(1)} %get-tuple-element.21), channel_id=1, source_target_pairs={{0,8},{8,0},{16,24},{24,16},{1,9},{9,1},{17,25},{25,17},{2,10},{10... | collective-permute-start | bytes 196616 | tf_op jit(solution)/shard_map/ppermute | solution.py:71
  89.3 19.7 %collective-permute-start.7 = (f32[8,4096]{1,0:T(8,128)}, f32[8,4096]{1,0:T(8,128)}, u32[]{:S(2)}, u32[]{:S(2)}) collective-permute-start(f32[8,4096]{1,0:T(8,128)} %maximum_select_fusion.3), channel_id=1, source_target_pairs={{0,16},{8,24},{16,0},{24,8},{1,17},{9,25},{17,1},{25,9},{2,18},{10... | collective-permute-start | bytes 393224 | tf_op jit(solution)/shard_map/ppermute | solution.py:71
  109.0 50.4 %copy-start.2 = (f32[4096]{0:T(1024)S(1)}, f32[4096]{0:T(1024)}, u32[]{:S(2)}) copy-start(f32[4096]{0:T(1024)} %param.14) | copy-start | bytes 49156
  111.6 4.0 %collective-permute-start.8 = (bf16[4,4,128]{2,0,1:T(4,128)(2,1)S(1)}, bf16[4,4,128]{2,0,1:T(4,128)(2,1)S(1)}, u32[]{:S(2)}, u32[]{:S(2)}) collective-permute-start(bf16[4,4,128]{2,0,1:T(4,128)(2,1)S(1)} %get-tuple-element.25), channel_id=1, source_target_pairs={{0,1},{1,2},{2,3},{3,4},{4,5},{5,6},{6,7},{8,9},{9,10},{10,11},{11... | collective-permute-start | bytes 12296 | tf_op jit(solution)/shard_map/ppermute | solution.py:20
  112.9 7.0 %collective-permute-start.9 = (bf16[4,4,128]{2,0,1:T(4,128)(2,1)S(1)}, bf16[4,4,128]{2,0,1:T(4,128)(2,1)S(1)}, u32[]{:S(2)}, u32[]{:S(2)}) collective-permute-start(bf16[4,4,128]{2,0,1:T(4,128)(2,1)S(1)} %get-tuple-element.26), channel_id=1, source_target_pairs={{1,0},{2,1},{3,2},{4,3},{5,4},{6,5},{7,6},{9,8},{10,9},{11,10},{12... | collective-permute-start | bytes 12296 | tf_op jit(solution)/shard_map/ppermute | solution.py:22
  124.3 34.4 %collective-permute-start.10 = (bf16[4,4,128]{2,0,1:T(4,128)(2,1)S(1)}, bf16[4,4,128]{2,0,1:T(4,128)(2,1)S(1)}, u32[]{:S(2)}, u32[]{:S(2)}) collective-permute-start(bf16[4,4,128]{2,0,1:T(4,128)(2,1)S(1)} %get-tuple-element.23), channel_id=1, source_target_pairs={{0,1},{1,2},{2,3},{3,4},{4,5},{5,6},{6,7},{8,9},{9,10},{10,11},{11... | collective-permute-start | bytes 12296 | tf_op jit(solution)/shard_map/ppermute | solution.py:20
  128.6 30.1 %collective-permute-start.11 = (bf16[4,4,128]{2,0,1:T(4,128)(2,1)S(1)}, bf16[4,4,128]{2,0,1:T(4,128)(2,1)S(1)}, u32[]{:S(2)}, u32[]{:S(2)}) collective-permute-start(bf16[4,4,128]{2,0,1:T(4,128)(2,1)S(1)} %get-tuple-element.24), channel_id=1, source_target_pairs={{1,0},{2,1},{3,2},{4,3},{5,4},{6,5},{7,6},{9,8},{10,9},{11,10},{12... | collective-permute-start | bytes 12296 | tf_op jit(solution)/shard_map/ppermute | solution.py:22
Sparse Core Ops, SparseCore 0:
  115.8 41.4 all-reduce.6
